TPU v7x, 32 devices: a whole 2x2x4 slice. The times are simulated.
32 devices in a mesh: line: 2 (over y), gather: 16 (over z, x, core).
Axes of the slice: x: 2, y: 2, z: 4, core: 2. Of those that a mesh axis runs over, the one named last changes fastest.
Arguments:
- noisy: bfloat16 [2, 16, 256, 256], P('line', 'gather'), may hold values from -6 to 6
- target: float32 [2, 16, 256, 256], P('line', None, 'gather'), may hold values from -6 to 6
- in_weight: bfloat16 [64, 4], replicated, may hold values from -3 to 3
- in_bias: float32 [64], replicated, may hold values from -3 to 3
- mid_weight: bfloat16 [3, 3, 64, 64], replicated, may hold values from -0.25 to 0.25
- mid_bias: float32 [64], replicated, may hold values from -3 to 3
- dec_weight: bfloat16 [3, 3, 64, 64], replicated, may hold values from -0.25 to 0.25
- dec_bias: float32 [64], replicated, may hold values from -3 to 3
- out_weight: bfloat16 [4, 64], replicated, may hold values from -0.75 to 0.75
- out_bias: float32 [4], replicated, may hold values from -3 to 3
Outputs:
- residual_map: float32 [2, 16, 256, 256], P('line', None, 'gather')
- in_weight_grad: float32 [64, 4], replicated
- in_bias_grad: float32 [64], replicated
- mid_weight_grad: float32 [3, 3, 64, 64], replicated
- mid_bias_grad: float32 [64], replicated
- dec_weight_grad: float32 [3, 3, 64, 64], replicated
- dec_bias_grad: float32 [64], replicated
- out_weight_grad: float32 [4, 64], replicated
- out_bias_grad: float32 [4], replicated
All inputs are finite; a program needn't handle non-finite values.
Results may differ from a plain program's by a relative error of at most 0.0014.
Values may be sent and summed in bfloat16 or wider, within the bound.
A program may use at most 128 MiB of HBM per device.

v0:
```python
import math

import jax
import jax.numpy as jnp
from jax import lax
from jax.sharding import PartitionSpec as P

R = 256
NT = 256


def conv_valid(inputs, weights, axis):
    count_rows = inputs.shape[axis] - 2
    steps_time = inputs.shape[3]
    channels = inputs.shape[2]
    padded = jnp.pad(inputs, ((0, 0), (0, 0), (0, 0), (1, 1)))
    stacked = jnp.concatenate([padded[..., tap : tap + steps_time] for tap in range(3)], axis=2)
    summed = None
    for row_tap in range(3):
        band_rows = lax.slice_in_dim(stacked, row_tap, row_tap + count_rows, axis=axis)
        flat_weights = weights[row_tap].transpose(1, 0, 2).reshape(weights.shape[2], 3 * channels)
        term = jnp.einsum(
            "dc,xyct->xydt", flat_weights, band_rows, preferred_element_type=jnp.float32
        )
        summed = term if summed is None else summed + term
    return summed


def first_layer(samples, in_weight, in_bias):
    shots_here, recv_here, time_here = samples.shape
    cells = samples.reshape(shots_here, recv_here // 2, 2, time_here // 2, 2)
    cells = cells.transpose(0, 1, 2, 4, 3).reshape(shots_here, recv_here // 2, 4, time_here // 2)
    pre_one = jnp.einsum("dk,arkt->ardt", in_weight, cells.astype(jnp.float32))
    pre_one = pre_one + in_bias[:, None]
    return jax.nn.silu(pre_one).astype(jnp.bfloat16)


def second_layer(rimmed, mid_weight, mid_bias):
    pre_two = conv_valid(rimmed, mid_weight, 1) + mid_bias[:, None]
    return jax.nn.silu(pre_two).astype(jnp.bfloat16)


def encoder(samples, in_weight, in_bias, mid_weight, mid_bias):
    hidden = first_layer(samples, in_weight, in_bias)
    rimmed = jnp.pad(hidden, ((0, 0), (1, 1), (0, 0), (0, 0)))
    return second_layer(rimmed, mid_weight, mid_bias)


def decoder(latent, dec_weight, dec_bias, out_weight, out_bias):
    padded = jnp.pad(latent, ((1, 1), (0, 0), (0, 0), (0, 0)))
    pre_three = conv_valid(padded, dec_weight, 0) + dec_bias[:, None]
    upper = jax.nn.silu(pre_three).astype(jnp.bfloat16)
    cells = jnp.einsum("kd,srdt->srkt", out_weight, upper.astype(jnp.float32))
    cells = cells + out_bias[:, None]
    shots_here, recv_here, four_taps, time_here = cells.shape
    cells = cells.reshape(shots_here, recv_here, 2, 2, time_here).transpose(0, 1, 2, 4, 3)
    return cells.reshape(shots_here, 2 * recv_here, 2 * time_here)


def per_device(
    noisy,
    target,
    in_weight,
    in_bias,
    mid_weight,
    mid_bias,
    dec_weight,
    dec_bias,
    out_weight,
    out_bias,
):
    line_count = lax.axis_size("line")
    shot_count = lax.axis_size("gather")
    loss_scale = 1.0 / math.sqrt(line_count * shot_count * R * NT)
    enc_params = tuple((p.astype(jnp.float32) for p in (in_weight, in_bias, mid_weight, mid_bias)))
    dec_params = tuple(
        (p.astype(jnp.float32) for p in (dec_weight, dec_bias, out_weight, out_bias))
    )
    shot_gather = noisy[0]
    truth_cols = target[0]
    latent, enc_pull = jax.vjp(lambda *params: encoder(shot_gather, *params), *enc_params)
    columns = lax.all_to_all(latent, "gather", split_axis=1, concat_axis=0, tiled=True)
    predicted, dec_pull = jax.vjp(decoder, columns, *dec_params)
    residual = predicted - truth_cols
    dec_cots = dec_pull(residual * loss_scale)
    returned = lax.all_to_all(dec_cots[0], "gather", split_axis=0, concat_axis=1, tiled=True)
    enc_grads = enc_pull(returned)
    summed = lax.psum(
        (
            enc_grads[0],
            enc_grads[1],
            enc_grads[2],
            enc_grads[3],
            dec_cots[1],
            dec_cots[2],
            dec_cots[3],
            dec_cots[4],
        ),
        ("line", "gather"),
    )
    return (
        residual[None],
        summed[0],
        summed[1],
        summed[2],
        summed[3],
        summed[4],
        summed[5],
        summed[6],
        summed[7],
    )


def solution(mesh):
    in_specs = (
        P("line", "gather", None, None),
        P("line", None, "gather", None),
        P(),
        P(),
        P(),
        P(),
        P(),
        P(),
        P(),
        P(),
    )
    out_specs = (P("line", None, "gather", None), P(), P(), P(), P(), P(), P(), P(), P())
    return jax.shard_map(
        per_device, mesh=mesh, in_specs=in_specs, out_specs=out_specs, check_vma=False
    )
```

profile of v0, /device:TPU:0, one launch (start us, length us, event | category | flops | bytes accessed | tf_op | source)
XLA Modules:
  0.0 369.1 jit_solution(4459387383840435962)
XLA Ops:
  8.4 19.9 %reshape_squeeze.3 = bf16[1,128,2,128,2]{4,3,2,1,0:T(8,128)(2,1)} reshape(bf16[1,1,256,256]{3,2,1,0:T(8,128)(2,1)} %param.10) | data formatting | bytes 262144 | tf_op jit(solution)/shard_map/jvp()/reshape;squeeze | solution.py:31
  28.3 7.1 %copy.98 = bf16[1,128,2,2,128]{4,1,3,2,0:T(8,128)(2,1)S(1)} copy(bf16[1,128,2,2,128]{3,4,2,1,0:T(8,128)(2,1)} %bitcast.351) | data formatting | bytes 262144 | tf_op jit(solution)/shard_map/jvp()/transpose | solution.py:32
  35.4 3.4 fusion.46
  50.3 8.0 %all-to-all-start = ((bf16[1,128,64,128]{3,2,0,1:T(8,128)(2,1)}), bf16[1,128,64,128]{3,2,0,1:T(8,128)(2,1)}, u32[]{:S(2)}, u32[]{:S(2)}) async-start(bf16[1,128,64,128]{3,2,0,1:T(8,128)(2,1)} %fusion.59), calls=%async_computation | async-start | bytes 4194304 | tf_op jit(solution)/shard_map/all_to_all | solution.py:82
  59.2 40.1 %all-to-all-done = bf16[1,128,64,128]{3,2,0,1:T(8,128)(2,1)} async-done(((bf16[1,128,64,128]{3,2,0,1:T(8,128)(2,1)}), bf16[1,128,64,128]{3,2,0,1:T(8,128)(2,1)}, u32[]{:S(2)}, u32[]{:S(2)}) %all-to-all-start) | async-done | bytes 2097184 | tf_op jit(solution)/shard_map/all_to_all | solution.py:82
  106.4 3.9 %fusion.48 = (bf16[16,8,64,128]{3,2,1,0:T(8,128)(2,1)S(1)}, f32[16,8,128,64]{2,3,1,0:T(8,128)}) fusion(f32[64]{0:T(128)S(1)} %copy-done.20, bf16[18,8,192,128]{3,2,1,0:T(8,128)(2,1)S(1)} %pad_maximum_fusion, bf16[64,192,1,1]{0,1,3,2:T(8,128)(2,1)S(1)} %bitcast.374, f32[16,8,128,64]{2,3,1,0:T(8,128)S(1)} %fusion.106, f32[16,8,128,64]{2,3,1,0:T(8,128)S(1)} %fusion.107), kind=kOutput, calls=%fused_computation.82 | convolution fusion | flops 411041792 | bytes 21782784 | tf_op jit(solution)/shard_map/jvp(dc,xyct->xydt)/dot_general | solution.py:22
  114.3 4.1 %fusion.90 = (f32[2,2]{1,0:T(2,128)S(1)}, bf16[16,8,2,2,128]{0,3,4,2,1:T(2,128)(2,1)S(1)}) fusion(f32[16,8,2,128,2]{0,4,3,2,1:T(2,128)S(1)} %bitcast.361, f32[16,8,2,2,128]{0,3,4,2,1:T(2,128)} %copy.113), kind=kLoop, calls=%fused_computation.117 | loop fusion | flops 262140 | bytes 655376 | tf_op jit(solution)/shard_map/transpose(jvp())/reduce_sum | solution.py:54
  119.8 5.6 %fusion.21 = (bf16[16,8,128,64]{2,3,1,0:T(8,128)(2,1)S(1)}, bf16[16,8,128,64]{2,3,1,0:T(8,128)(2,1)}) fusion(f32[16,8,128,64]{2,3,1,0:T(8,128)} %get-tuple-element.72, bf16[4,64]{1,0:T(4,128)(2,1)S(1)} %copy-done, bf16[16,8,128,4]{2,1,3,0:T(8,128)(2,1)} %bitcast.378), kind=kOutput, calls=%fused_computation.46 | convolution fusion | flops 19922944 | bytes 8520192 | tf_op jit(solution)/shard_map/transpose(jvp(kd,srdt->srkt))/dot_general | solution.py:53
  131.7 2.6 fusion.96
  134.4 2.8 pad_add_fusion.4
  137.2 11.3 %all-to-all-start.1 = ((bf16[16,8,64,128]{3,2,1,0:T(8,128)(2,1)}), bf16[16,8,64,128]{3,2,1,0:T(8,128)(2,1)}, u32[]{:S(2)}, u32[]{:S(2)}) async-start(bf16[16,8,64,128]{3,2,1,0:T(8,128)(2,1)} %pad_add_fusion.4), calls=%async_computation.1 | async-start | bytes 4194304 | tf_op jit(solution)/shard_map/all_to_all | solution.py:86
  148.5 16.3 %fusion.97 = (bf16[1,128,192,128]{3,2,1,0:T(8,128)(2,1)}, bf16[1,128,192,128]{3,2,1,0:T(8,128)(2,1)}, bf16[1,128,192,128]{3,2,1,0:T(8,128)(2,1)}) fusion(bf16[1,130,192,128]{3,2,1,0:T(8,128)(2,1)} %copy-done.2), kind=kLoop, calls=%fused_computation.121 | loop fusion | bytes 37748736 | tf_op jit(solution)/shard_map/jvp()/slice | solution.py:20
  164.8 3.4 sub.21
  168.2 3.1 copy.132
  171.3 5.3 %fusion = f32[64,192,1,1]{0,1,3,2:T(8,128)S(1)} fusion(bf16[16,8,128,64]{2,3,1,0:T(8,128)(2,1)} %copy-done.5, bf16[18,8,192,128]{3,2,1,0:T(8,128)(2,1)} %copy-done.3), kind=kOutput, calls=%fused_computation.4 | convolution fusion | flops 402653184 | bytes 8437760 | tf_op jit(solution)/shard_map/transpose(jvp(dc,xyct->xydt))/dot_general | solution.py:22
  183.8 5.9 %all-to-all-done.1 = bf16[16,8,64,128]{3,2,1,0:T(8,128)(2,1)} async-done(((bf16[16,8,64,128]{3,2,1,0:T(8,128)(2,1)}), bf16[16,8,64,128]{3,2,1,0:T(8,128)(2,1)}, u32[]{:S(2)}, u32[]{:S(2)}) %all-to-all-start.1) | async-done | bytes 2097184 | tf_op jit(solution)/shard_map/all_to_all | solution.py:86
  189.6 4.1 %fusion.92 = (f32[64]{0:T(128)S(1)}, bf16[1,128,64,128]{3,2,1,0:T(8,128)(2,1)S(1)}) fusion(f32[1,128,128,64]{2,3,1,0:T(8,128)} %copy-done.4, bf16[1,128,64,128]{3,2,1,0:T(8,128)(2,1)} %bitcast.302.clone.2), kind=kLoop, calls=%fused_computation.118 | loop fusion | flops 12582848 | bytes 8388864 | tf_op jit(solution)/shard_map/transpose(jvp())/reduce_sum | solution.py:39
  195.5 4.4 %convert_bitcast_fusion.1 = bf16[1,128,192,128]{3,2,1,0:T(8,128)(2,1)} fusion(bf16[64,192,1]{0,1,2:T(8,128)(2,1)S(1)} %bitcast.369, bf16[1,128,64,128]{3,2,1,0:T(8,128)(2,1)S(1)} %get-tuple-element.47), kind=kOutput, calls=%fused_computation.19 | convolution fusion | flops 402653184 | bytes 8413184 | tf_op jit(solution)/shard_map/transpose(jvp(dc,xyct->xydt))/dot_general | solution.py:22
  199.9 4.7 %convert_bitcast_fusion.2 = bf16[1,128,192,128]{3,2,1,0:T(8,128)(2,1)} fusion(bf16[64,192,1]{0,1,2:T(8,128)(2,1)S(1)} %bitcast.365, bf16[1,128,64,128]{3,2,1,0:T(8,128)(2,1)S(1)} %get-tuple-element.47), kind=kOutput, calls=%fused_computation.20 | convolution fusion | flops 402653184 | bytes 8413184 | tf_op jit(solution)/shard_map/transpose(jvp(dc,xyct->xydt))/dot_general | solution.py:22
  204.6 6.2 %pad_add_fusion.1 = bf16[1,130,192,128]{3,2,1,0:T(8,128)(2,1)S(1)} fusion(bf16[1,128,192,128]{3,2,1,0:T(8,128)(2,1)S(1)} %convert_bitcast_fusion, bf16[1,128,192,128]{3,2,1,0:T(8,128)(2,1)} %convert_bitcast_fusion.1, bf16[1,128,192,128]{3,2,1,0:T(8,128)(2,1)} %convert_bitcast_fusion.2), kind=kLoop, calls=%fused_computation.3 | loop fusion | flops 6389760 | bytes 25264128 | tf_op jit(solution)/shard_map/transpose(jvp())/add_any | solution.py:20
  210.9 4.0 %fusion.98 = (bf16[1,130,64,128]{3,2,1,0:T(8,128)(2,1)S(1)}, bf16[1,130,64,128]{3,2,1,0:T(8,128)(2,1)}, bf16[1,130,64,128]{3,2,1,0:T(8,128)(2,1)}) fusion(bf16[1,130,192,128]{3,2,1,0:T(8,128)(2,1)S(1)} %pad_add_fusion.1), kind=kLoop, calls=%fused_computation.122 | loop fusion | bytes 12779520 | tf_op jit(solution)/shard_map/transpose(jvp())/split | solution.py:17
  223.5 5.7 %fusion.94 = (f32[64]{0:T(128)S(1)}, bf16[1,128,64,128]{3,2,1,0:T(8,128)(2,1)S(1)}) fusion(f32[64]{0:T(128)S(1)} %copy-done.18, f32[128,128,64]{1,2,0:T(8,128)} %get-tuple-element.70, bf16[1,130,64,128]{3,2,1,0:T(8,128)(2,1)} %get-tuple-element.57, bf16[1,130,64,128]{3,2,1,0:T(8,128)(2,1)} %get-tuple-element.58, ...), kind=kLoop, calls=%fused_computation.119 | loop fusion | flops 18874304 | bytes 12681728 | tf_op jit(solution)/shard_map/transpose(jvp())/reduce_sum | solution.py:34
  229.9 46.9 %all-reduce.24 = (f32[64,4]{0,1:T(4,128)}, f32[64]{0:T(128)}, f32[64]{0:T(128)}, f32[64]{0:T(128)}, f32[4,64]{1,0:T(4,128)}, /*index=5*/f32[4]{0:T(128)}) all-reduce(f32[64,4]{0,1:T(4,128)S(1)} %fusion.69, f32[64]{0:T(128)S(1)} %get-tuple-element.48, ...), channel_id=1, replica_groups=mesh['line'=2,'gather'=16] {'line','gather'}, use_global_device_ids=true, to_apply=%region_0.1 | all-reduce | flops 708 | bytes 5664 | tf_op jit(solution)/shard_map/psum | solution.py:88
  276.7 81.4 %all-reduce.28.cloned.1.call-done = (f32[3,3,64,64]{3,2,1,0:T(8,128)}, f32[3,3,64,64]{2,3,1,0:T(8,128)}) async-done(((f32[3,3,64,64]{3,2,1,0:T(8,128)}, f32[3,3,64,64]{2,3,1,0:T(8,128)}), (f32[3,3,64,64]{3,2,1,0:T(8,128)}, f32[3,3,64,64]{2,3,1,0:T(8,128)})) %all-reduce.28.cloned.1.call-update) | async-done | bytes 294928 | tf_op jit(solution)/shard_map/psum | solution.py:88
  (106 shorter events, 53.7 us)
Async XLA Ops:
  7.2 104.4 %copy-start = (bf16[4,64]{1,0:T(4,128)(2,1)S(1)}, bf16[4,64]{1,0:T(4,128)(2,1)}, u32[]{:S(2)}) copy-start(bf16[4,64]{1,0:T(4,128)(2,1)} %param.18) | copy-start | bytes 1540
  28.3 7.1 %copy-start.18 = (f32[64]{0:T(128)S(1)}, f32[64]{0:T(128)}, u32[]{:S(2)}) copy-start(f32[64]{0:T(128)} %param.13) | copy-start | bytes 772
  28.3 7.2 %copy-start.19 = (bf16[64,4]{0,1:T(4,128)(2,1)S(1)}, bf16[64,4]{0,1:T(4,128)(2,1)}, u32[]{:S(2)}) copy-start(bf16[64,4]{0,1:T(4,128)(2,1)} %param.12) | copy-start | bytes 1540
  35.4 3.5 copy-start.13
  47.8 10.4 %copy-start.12 = (bf16[3,3,64,64]{3,2,1,0:T(8,128)(2,1)S(1)}, bf16[3,3,64,64]{3,2,1,0:T(8,128)(2,1)}, u32[]{:S(2)}) copy-start(bf16[3,3,64,64]{3,2,1,0:T(8,128)(2,1)} %param.16) | copy-start | bytes 221188
  47.8 10.8 %copy-start.11 = (f32[1,16,16,256]{3,2,1,0:T(8,128)S(1)}, f32[1,16,16,256]{3,2,1,0:T(8,128)}, u32[]{:S(2)}) copy-start(f32[1,16,16,256]{3,2,1,0:T(8,128)} %param.11) | copy-start | bytes 786436
  50.3 49.1 %all-to-all-start = ((bf16[1,128,64,128]{3,2,0,1:T(8,128)(2,1)}), bf16[1,128,64,128]{3,2,0,1:T(8,128)(2,1)}, u32[]{:S(2)}, u32[]{:S(2)}) async-start(bf16[1,128,64,128]{3,2,0,1:T(8,128)(2,1)} %fusion.59), calls=%async_computation | async-start | bytes 4194304 | tf_op jit(solution)/shard_map/all_to_all | solution.py:82
  103.5 2.9 copy-start.3
  106.4 5.2 %copy-start.17 = (f32[4]{0:T(128)S(1)}, f32[4]{0:T(128)}, u32[]{:S(2)}) copy-start(f32[4]{0:T(128)} %param.19) | copy-start | bytes 52
  125.4 3.6 copy-start.5
  137.2 52.4 %all-to-all-start.1 = ((bf16[16,8,64,128]{3,2,1,0:T(8,128)(2,1)}), bf16[16,8,64,128]{3,2,1,0:T(8,128)(2,1)}, u32[]{:S(2)}, u32[]{:S(2)}) async-start(bf16[16,8,64,128]{3,2,1,0:T(8,128)(2,1)} %pad_add_fusion.4), calls=%async_computation.1 | async-start | bytes 4194304 | tf_op jit(solution)/shard_map/all_to_all | solution.py:86
  148.5 209.7 %all-reduce.28.cloned.1.call-start = ((), (), s32[]{:S(2)}) async-start(), calls=%async_computation.2 | async-start | bytes 1179648 | tf_op jit(solution)/shard_map/psum | solution.py:88
  168.2 8.4 %slice-start = ((s8[7077888]{0:T(1024)(128)(4,1)}), s8[2883584]{0:T(1024)(128)(4,1)S(1)}, s32[]{:S(2)}) async-start(s8[7077888]{0:T(1024)(128)(4,1)} %bitcast.349), calls=%async_computation.3 | async-start | bytes 5767168
  171.3 5.3 %slice-start.1 = ((s8[7077888]{0:T(1024)(128)(4,1)}), s8[4194304]{0:T(1024)(128)(4,1)S(1)}, s32[]{:S(2)}) async-start(s8[7077888]{0:T(1024)(128)(4,1)} %bitcast.349), calls=%async_computation.4 | async-start | bytes 8388608
  171.3 5.4 %copy-start.6 = (bf16[16,8,128,64]{2,3,1,0:T(8,128)(2,1)S(1)}, bf16[16,8,128,64]{2,3,1,0:T(8,128)(2,1)}, u32[]{:S(2)}) copy-start(bf16[16,8,128,64]{2,3,1,0:T(8,128)(2,1)} %copy-done.5) | copy-start | bytes 6291460
  178.5 3.2 copy-start.7
  178.5 3.6 copy-start.8
  199.9 14.9 %slice-start.6 = ((s8[6291456]{0:T(1024)(128)(4,1)}), s8[4194304]{0:T(1024)(128)(4,1)S(1)}, s32[]{:S(2)}) async-start(s8[6291456]{0:T(1024)(128)(4,1)} %bitcast.358), calls=%async_computation.9 | async-start | bytes 8388608
  199.9 17.5 %slice-start.4 = ((s8[6291456]{0:T(1024)(128)(4,1)}), s8[4194304]{0:T(1024)(128)(4,1)S(1)}, s32[]{:S(2)}) async-start(s8[6291456]{0:T(1024)(128)(4,1)} %bitcast.355), calls=%async_computation.7 | async-start | bytes 8388608
  204.6 10.3 %slice-start.7 = ((s8[6291456]{0:T(1024)(128)(4,1)}), s8[2097152]{0:T(1024)(128)(4,1)S(1)}, s32[]{:S(2)}) async-start(s8[6291456]{0:T(1024)(128)(4,1)} %bitcast.358), calls=%async_computation.10 | async-start | bytes 4194304
  204.6 12.9 %slice-start.5 = ((s8[6291456]{0:T(1024)(128)(4,1)}), s8[2097152]{0:T(1024)(128)(4,1)S(1)}, s32[]{:S(2)}) async-start(s8[6291456]{0:T(1024)(128)(4,1)} %bitcast.355), calls=%async_computation.8 | async-start | bytes 4194304
  214.9 5.2 %slice-start.2 = ((s8[6291456]{0:T(1024)(128)(4,1)}), s8[4194304]{0:T(1024)(128)(4,1)S(1)}, s32[]{:S(2)}) async-start(s8[6291456]{0:T(1024)(128)(4,1)} %bitcast.352), calls=%async_computation.5 | async-start | bytes 8388608
  223.5 5.7 %copy-start.14 = (bf16[1,128,2,2,128]{4,1,3,2,0:T(8,128)(2,1)S(1)}, bf16[1,128,2,2,128]{4,1,3,2,0:T(8,128)(2,1)}, u32[]{:S(2)}) copy-start(bf16[1,128,2,2,128]{4,1,3,2,0:T(8,128)(2,1)} %copy-done.13) | copy-start | bytes 393220
  223.5 138.2 %copy-start.1 = (bf16[4,64]{1,0:T(4,128)(2,1)S(1)}, bf16[4,64]{1,0:T(4,128)(2,1)}, u32[]{:S(2)}) copy-start(bf16[4,64]{1,0:T(4,128)(2,1)} %param.18) | copy-start | bytes 1540
  (8 other events, 16.7 us)
Sparse Core Ops, SparseCore 0:
  223.6 134.5 all-reduce.27
where the time goes:
time: 376 us; the launch traced here: 369 us
  waiting for transfers between devices  127 us (34%)
  local copies, waits for them, and re-layouts  71.5 us (19%)
  matrix products  54.3 us (14%)
  blocking collectives  46.9 us (12%)
  other arithmetic  34.7 us (9%)
  starting transfers between devices  19.3 us (5%)
  between operations  15.1 us (4%)
    psum x1, waiting for transfers between devices, per_device(): lax.psum((enc_grads[0], enc_grads[1], enc_grads[2], enc_grads[3], dec_cot...  81.4 us
    psum x1, blocking collectives, per_device(): lax.psum((enc_grads[0], enc_grads[1], enc_grads[2], enc_grads[3], dec_cot...  46.9 us
    dot_general x18, matrix products, conv_valid(): jnp.einsum('dc,xyct->xydt', flat_weights, band_rows, preferred_element_ty...  43.6 us
    all_to_all x1, waiting for transfers between devices, per_device(): lax.all_to_all(latent, 'gather', split_axis=1, concat_axis=0, tiled=True)  40.1 us
    another operation x1, local copies, waits for them, and re-layouts, first_layer(): cells = samples.reshape(shots_here, recv_here // 2, 2, time_here // 2, 2)  19.9 us
    slice x1, local copies, waits for them, and re-layouts, conv_valid(): lax.slice_in_dim(stacked, row_tap, row_tap + count_rows, axis=axis)  16.3 us
    unnamed x62, local copies, waits for them, and re-layouts  11.3 us
    all_to_all x1, starting transfers between devices, per_device(): lax.all_to_all(dec_cots[0], 'gather', split_axis=0, concat_axis=1, tiled=...  11.3 us
  transfers between devices with their start and end apart: 3, of which 3 were waited for; matrix products, arithmetic and copies ran while one was open for 11% of the time, Pallas kernels for 0%

commit v1 on v0

v1 whole, which is shorter than its diff:
```python
import functools
import math

import jax
import jax.numpy as jnp
from jax import lax
from jax.experimental import pallas as pl
from jax.experimental.pallas import tpu as pltpu
from jax.sharding import PartitionSpec as P

MESH = pl.DeviceIdType.MESH
BF = jnp.bfloat16
F32 = jnp.float32


def exchange_kernel(n, x_ref, out_ref, held, send_sem, recv_sem):
    line = lax.axis_index("line")
    me = lax.axis_index("gather")
    barrier = pltpu.get_barrier_semaphore()

    def greet(k, carry):
        peer = lax.rem(me + k, n)
        pl.semaphore_signal(barrier, inc=1, device_id=(line, peer), device_id_type=MESH)
        return carry

    lax.fori_loop(1, n, greet, 0)
    pl.semaphore_wait(barrier, n - 1)

    def copy(src, slot, peer, sem):
        return pltpu.make_async_remote_copy(
            src_ref=x_ref.at[src],
            dst_ref=held.at[slot],
            send_sem=send_sem.at[sem],
            recv_sem=recv_sem.at[slot],
            device_id=(line, peer),
            device_id_type=MESH,
        )

    def send(k, carry):
        peer = lax.rem(me + k, n)
        copy(peer, me, peer, k).start()
        return carry

    lax.fori_loop(1, n, send, 0)
    out_ref[pl.ds(me, 1)] = x_ref[pl.ds(me, 1)]

    def finish(k, carry):
        peer = lax.rem(me + k, n)
        source = lax.rem(me + n - k, n)
        copy(peer, source, peer, k).wait_recv()
        copy(peer, source, peer, k).wait_send()
        out_ref[pl.ds(source, 1)] = held[pl.ds(source, 1)]
        return carry

    lax.fori_loop(1, n, finish, 0)


def exchange(x):
    n = x.shape[0]
    return pl.pallas_call(
        functools.partial(exchange_kernel, n),
        out_shape=jax.ShapeDtypeStruct(x.shape, x.dtype),
        in_specs=[pl.BlockSpec(memory_space=pltpu.VMEM)],
        out_specs=pl.BlockSpec(memory_space=pltpu.VMEM),
        scratch_shapes=[
            pltpu.VMEM(x.shape, x.dtype),
            pltpu.SemaphoreType.DMA((n,)),
            pltpu.SemaphoreType.DMA((n,)),
        ],
        compiler_params=pltpu.CompilerParams(
            collective_id=0, has_side_effects=True, vmem_limit_bytes=16 << 20
        ),
    )(x)


def total_kernel(nd, n, x_ref, out_ref, held, result, send_sem, recv_sem, back_sem, done_sem):
    me = lax.axis_index("line") * n + lax.axis_index("gather")

    def at(peer):
        return (peer // n, lax.rem(peer, n))

    barrier = pltpu.get_barrier_semaphore()

    def greet(k, carry):
        peer = lax.rem(me + k, nd)
        pl.semaphore_signal(barrier, inc=1, device_id=at(peer), device_id_type=MESH)
        return carry

    lax.fori_loop(1, nd, greet, 0)
    pl.semaphore_wait(barrier, nd - 1)

    def part(src, slot, peer, sem):
        return pltpu.make_async_remote_copy(
            src_ref=x_ref.at[src],
            dst_ref=held.at[slot],
            send_sem=send_sem.at[sem],
            recv_sem=recv_sem.at[slot],
            device_id=at(peer),
            device_id_type=MESH,
        )

    def whole(slot, peer, sem):
        return pltpu.make_async_remote_copy(
            src_ref=result.at[slot],
            dst_ref=result.at[slot],
            send_sem=back_sem.at[sem],
            recv_sem=done_sem.at[slot],
            device_id=at(peer),
            device_id_type=MESH,
        )

    def send(k, carry):
        peer = lax.rem(me + k, nd)
        part(peer, me, peer, k).start()
        return carry

    lax.fori_loop(1, nd, send, 0)

    def add(k, acc):
        source = lax.rem(me + nd - k, nd)
        part(source, source, source, k).wait_recv()
        return acc + held[pl.ds(source, 1)]

    result[pl.ds(me, 1)] = lax.fori_loop(1, nd, add, x_ref[pl.ds(me, 1)])

    def spread(k, carry):
        peer = lax.rem(me + k, nd)
        whole(me, peer, k).start()
        return carry

    lax.fori_loop(1, nd, spread, 0)

    def finish(k, carry):
        peer = lax.rem(me + k, nd)
        source = lax.rem(me + nd - k, nd)
        part(peer, me, peer, k).wait_send()
        whole(me, peer, k).wait_send()
        whole(source, peer, k).wait_recv()
        return carry

    lax.fori_loop(1, nd, finish, 0)
    out_ref[...] = result[...]


def total(x, n):
    nd = x.shape[0]
    sems = pltpu.SemaphoreType.DMA((nd,))
    return pl.pallas_call(
        functools.partial(total_kernel, nd, n),
        out_shape=jax.ShapeDtypeStruct(x.shape, x.dtype),
        in_specs=[pl.BlockSpec(memory_space=pltpu.VMEM)],
        out_specs=pl.BlockSpec(memory_space=pltpu.VMEM),
        scratch_shapes=[
            pltpu.VMEM(x.shape, x.dtype),
            pltpu.VMEM(x.shape, x.dtype),
            sems,
            sems,
            sems,
            sems,
        ],
        compiler_params=pltpu.CompilerParams(
            collective_id=1, has_side_effects=True, vmem_limit_bytes=16 << 20
        ),
    )(x)


def gate(pre):
    sig = 1.0 / (1.0 + jnp.exp(-pre))
    act = pre * sig
    return act, sig + act * (1.0 - sig)


def dot(a, b):
    return jnp.dot(a, b, preferred_element_type=F32)


def dot_t(a, b):
    return lax.dot_general(a, b, (((1,), (1,)), ((), ())), preferred_element_type=F32)


def exact_dot(x, onehot):
    hi = x.astype(BF)
    rest = x - hi.astype(F32)
    mid = rest.astype(BF)
    low = (rest - mid.astype(F32)).astype(BF)
    return dot(hi, onehot) + dot(mid, onehot) + dot(low, onehot)


def step_kernel(
    scale,
    a_ref,
    target_ref,
    win_ref,
    w2_ref,
    w3_ref,
    v2_ref,
    v3_ref,
    wout_ref,
    woutt_ref,
    ib_ref,
    mb_ref,
    db_ref,
    ob_ref,
    edge_ref,
    deint_ref,
    inter_ref,
    res_ref,
    g2_ref,
    g3_ref,
    gin_ref,
    gout_ref,
    gob_ref,
    gmb_ref,
    gdb_ref,
    h_ref,
    z_ref,
    e3_ref,
    e2_ref,
    e1_ref,
    h3_ref,
    s1_ref,
    s2_ref,
    s3_ref,
):
    shots, rows = target_ref.shape[0], target_ref.shape[1]
    rl = rows // 2
    hr = rl + 2
    c = ib_ref.shape[0]
    t = ib_ref.shape[1]
    lane = lax.broadcasted_iota(jnp.int32, (c, t), 1)
    first, last = lane == 0, lane == t - 1

    def later(x):
        return jnp.where(first, 0.0, pltpu.roll(x, 1, 1)).astype(BF)

    def sooner(x):
        return jnp.where(last, 0.0, pltpu.roll(x, t - 1, 1)).astype(BF)

    def band(ref, r):
        return ref[r : r + 3].reshape(3 * 3 * c, t)

    for r in range(rl):
        for slot in (0, shots + 1):
            z_ref[r, slot] = jnp.zeros((3 * c, t), BF)
            e3_ref[r, slot] = jnp.zeros((3 * c, t), BF)
    for slot in (0, 1, rl + 2, rl + 3):
        e2_ref[slot] = jnp.zeros((3 * c, t), BF)
    for ref in (g2_ref, g3_ref, gin_ref, gout_ref, gob_ref, gmb_ref, gdb_ref):
        ref[...] = jnp.zeros_like(ref)

    def encode(s, carry):
        pre1 = dot(win_ref[...], a_ref[s])
        for r in range(hr):
            act, slope = gate(pre1[r * c : (r + 1) * c] + ib_ref[...])
            if r == 0:
                act, slope = act * edge_ref[0:1], slope * edge_ref[0:1]
            if r == hr - 1:
                act, slope = act * edge_ref[1:2], slope * edge_ref[1:2]
            s1_ref[s, r] = slope
            h_ref[s, r, 0:c] = later(act)
            h_ref[s, r, c : 2 * c] = act.astype(BF)
            h_ref[s, r, 2 * c : 3 * c] = sooner(act)
        for r in range(0, rl, 2):
            wide = jnp.concatenate(
                [h_ref[s, r + q : r + q + 3].reshape(9 * c, t) for q in range(2)], axis=1
            )
            pre2 = dot(w2_ref[...], wide)
            for q in range(2):
                act, slope = gate(pre2[:, q * t : (q + 1) * t] + mb_ref[...])
                s2_ref[s, r + q] = slope
                z_ref[r + q, s + 1, 0:c] = later(act)
                z_ref[r + q, s + 1, c : 2 * c] = act.astype(BF)
                z_ref[r + q, s + 1, 2 * c : 3 * c] = sooner(act)
        return carry

    lax.fori_loop(0, shots, encode, 0)

    def decode(s, carry):
        for r in range(0, rl, 2):
            wide = jnp.concatenate(
                [z_ref[r + q, pl.ds(s, 3)].reshape(9 * c, t) for q in range(2)], axis=1
            )
            pre3 = dot(w3_ref[...], wide)
            for q in range(2):
                act, slope = gate(pre3[:, q * t : (q + 1) * t] + db_ref[...])
                s3_ref[r + q] = slope
                h3_ref[(r + q) * c : (r + q + 1) * c] = act.astype(BF)
        truth = exact_dot(target_ref[s], deint_ref[...])
        truth = jnp.concatenate([truth[:, :t], truth[:, t:]], axis=0)
        resid = dot(wout_ref[...], h3_ref[...]) + ob_ref[...] - truth
        side = jnp.concatenate([resid[:rows], resid[rows:]], axis=1)
        res_ref[s] = exact_dot(side, inter_ref[...])
        g = resid * scale
        gob_ref[...] += g
        g = g.astype(BF)
        gout_ref[...] += dot_t(g, h3_ref[...])
        back3 = dot(woutt_ref[...], g)
        bias = gdb_ref[...]
        for r in range(rl):
            e = back3[r * c : (r + 1) * c].astype(BF).astype(F32) * s3_ref[r]
            bias = bias + e
            e3_ref[r, s + 1, 0:c] = sooner(e)
            e3_ref[r, s + 1, c : 2 * c] = e.astype(BF)
            e3_ref[r, s + 1, 2 * c : 3 * c] = later(e)
        gdb_ref[...] = bias
        left = jnp.concatenate([e3_ref[r, s + 1] for r in range(rl)], axis=1)
        right = jnp.concatenate(
            [z_ref[r, pl.ds(s, 3), c : 2 * c].reshape(3 * c, t) for r in range(rl)], axis=1
        )
        g3_ref[...] += dot_t(left, right)
        return carry

    lax.fori_loop(0, shots, decode, 0)

    def pull(s, carry):
        bias = gmb_ref[...]
        for r in range(0, rl, 2):
            wide = jnp.concatenate(
                [e3_ref[r + q, pl.ds(s, 3)].reshape(9 * c, t) for q in range(2)], axis=1
            )
            back2 = dot(v3_ref[...], wide)
            for q in range(2):
                e = back2[:, q * t : (q + 1) * t].astype(BF).astype(F32) * s2_ref[s, r + q]
                bias = bias + e
                e2_ref[r + q + 2, 0:c] = sooner(e)
                e2_ref[r + q + 2, c : 2 * c] = e.astype(BF)
                e2_ref[r + q + 2, 2 * c : 3 * c] = later(e)
        gmb_ref[...] = bias
        left = jnp.concatenate([e2_ref[r + 2] for r in range(rl)], axis=1)
        right = jnp.concatenate(
            [h_ref[s, r : r + 3, c : 2 * c].reshape(3 * c, t) for r in range(rl)], axis=1
        )
        g2_ref[...] += dot_t(left, right)
        for r in range(0, hr, 2):
            wide = jnp.concatenate(
                [e2_ref[r + q : r + q + 3].reshape(9 * c, t) for q in range(2)], axis=1
            )
            back1 = dot(v2_ref[...], wide)
            for q in range(2):
                e = back1[:, q * t : (q + 1) * t].astype(BF).astype(F32) * s1_ref[s, r + q]
                e1_ref[(r + q) * c : (r + q + 1) * c] = e.astype(BF)
        gin_ref[...] += dot_t(e1_ref[...], a_ref[s])
        return carry

    lax.fori_loop(0, shots, pull, 0)


def step(scale, operands, shots, rows, c, t, ka):
    rl = rows // 2
    hr = rl + 2
    vmem = pl.BlockSpec(memory_space=pltpu.VMEM)
    shape = jax.ShapeDtypeStruct
    outs = (
        shape((shots, rows, 2 * t), F32),
        shape((3 * c, 3 * c), F32),
        shape((3 * c, 3 * c), F32),
        shape((hr * c, ka), F32),
        shape((2 * rows, rl * c), F32),
        shape((2 * rows, t), F32),
        shape((c, t), F32),
        shape((c, t), F32),
    )
    flops = 2 * 6 * 9 * c * c * shots * rl * t
    return pl.pallas_call(
        functools.partial(step_kernel, scale),
        out_shape=outs,
        in_specs=[vmem] * len(operands),
        out_specs=(vmem,) * len(outs),
        scratch_shapes=[
            pltpu.VMEM((shots, hr, 3 * c, t), BF),
            pltpu.VMEM((rl, shots + 2, 3 * c, t), BF),
            pltpu.VMEM((rl, shots + 2, 3 * c, t), BF),
            pltpu.VMEM((rl + 4, 3 * c, t), BF),
            pltpu.VMEM((hr * c, t), BF),
            pltpu.VMEM((rl * c, t), BF),
            pltpu.VMEM((shots, hr, c, t), F32),
            pltpu.VMEM((shots, rl, c, t), F32),
            pltpu.VMEM((rl, c, t), F32),
        ],
        compiler_params=pltpu.CompilerParams(vmem_limit_bytes=56 << 20),
        cost_estimate=pl.CostEstimate(
            flops=flops, bytes_accessed=8 << 20, transcendentals=3 * c * shots * rl * t
        ),
    )(*operands)


def per_device(noisy, target, in_w, in_b, mid_w, mid_b, dec_w, dec_b, out_w, out_b):
    lines, n = lax.axis_size("line"), lax.axis_size("gather")
    nd = lines * n
    recv, nt = noisy.shape[2], noisy.shape[3]
    shots, rows = target.shape[1], target.shape[2]
    c, t, rl = in_w.shape[0], nt // 2, rows // 2
    hr = rl + 2
    scale = 1.0 / math.sqrt(lines * n * recv * nt)
    me = lax.axis_index("gather")
    ka = -(-(4 * hr + 1) // 16) * 16

    when = jnp.arange(nt)
    deint = (when[:, None] == (2 * (when % t) + when // t)[None, :]).astype(BF)
    inter = deint.T
    wanted = (jnp.arange(n)[:, None] * rows + jnp.arange(2 * hr)[None, :] - 2).reshape(-1)
    select = (wanted[:, None] == jnp.arange(recv)[None, :]).astype(BF)
    picked = dot(select, noisy[0, 0]).astype(BF)
    picked = dot(picked, deint).astype(BF).reshape(n, 2 * hr, nt)
    tail = jnp.zeros((n, ka - 4 * hr, t), BF).at[:, 0].set(1.0)
    blocks = jnp.concatenate([picked[..., :t], picked[..., t:], tail], axis=1)
    cells = exchange(blocks)

    iw = in_w.reshape(c, 2, 2)
    win = jnp.einsum("rq,dij->rdjqi", jnp.eye(hr, dtype=BF), iw).reshape(hr * c, 4 * hr)
    win = jnp.pad(win, ((0, 0), (0, ka - 4 * hr)))
    ow = out_w.reshape(2, 2, c)
    wout = jnp.einsum("rq,ijd->jqird", jnp.eye(rl, dtype=BF), ow).reshape(2 * rows, rl * c)
    ob = jnp.broadcast_to(out_b.reshape(2, 2).T[:, None, :], (2, rl, 2)).reshape(2 * rows, 1)
    w2 = mid_w.transpose(2, 0, 1, 3).reshape(c, 9 * c)
    w3 = dec_w.transpose(2, 0, 1, 3).reshape(c, 9 * c)
    v2 = mid_w[::-1].transpose(3, 0, 1, 2).reshape(c, 9 * c)
    v3 = dec_w[::-1].transpose(3, 0, 1, 2).reshape(c, 9 * c)
    edge = jnp.stack([me > 0, me < n - 1]).astype(F32)
    operands = (
        cells,
        target[0],
        win,
        w2,
        w3,
        v2,
        v3,
        wout,
        wout.T,
        jnp.broadcast_to(in_b[:, None], (c, t)),
        jnp.broadcast_to(mid_b[:, None], (c, t)),
        jnp.broadcast_to(dec_b[:, None], (c, t)),
        jnp.broadcast_to(ob, (2 * rows, t)),
        jnp.broadcast_to(edge[:, None], (2, t)),
        deint,
        inter,
    )
    res, g2, g3, gin, gout, gob, gmb, gdb = step(scale, operands, shots, rows, c, t, ka)

    gin_w = jnp.einsum("rdjri->dij", gin[:, : 4 * hr].reshape(hr, c, 2, hr, 2)).reshape(c, 4)
    gin_b = gin[:, 4 * hr].reshape(hr, c).sum(0)
    gout_w = jnp.einsum("jrird->ijd", gout.reshape(2, rl, 2, rl, c)).reshape(4, c)
    gout_b = gob.sum(1).reshape(2, rl, 2).sum(1).T.reshape(4)
    small = jnp.concatenate(
        [gin_w.reshape(-1), gin_b, gmb.sum(1), gdb.sum(1), gout_w.reshape(-1), gout_b]
    )
    flat = jnp.concatenate([g2.reshape(-1), g3.reshape(-1), small])
    per = -(-flat.shape[0] // (nd * 8 * 128)) * 8
    flat = jnp.pad(flat, (0, nd * per * 128 - flat.shape[0])).reshape(nd, per, 128)
    flat = total(flat, n).reshape(-1)

    def taps(part):
        return part.reshape(3, c, 3, c).transpose(2, 0, 1, 3)

    big = 9 * c * c
    at = [2 * big]

    def take(count):
        at[0] += count
        return flat[at[0] - count : at[0]]

    din_w = take(4 * c).reshape(c, 4)
    din_b, dmid_b, ddec_b = take(c), take(c), take(c)
    dout_w = take(4 * c).reshape(4, c)
    dout_b = take(4)
    return (
        res[None],
        din_w,
        din_b,
        taps(flat[:big]),
        dmid_b,
        taps(flat[big : 2 * big]),
        ddec_b,
        dout_w,
        dout_b,
    )


def solution(mesh):
    in_specs = (
        P("line", "gather", None, None),
        P("line", None, "gather", None),
        P(),
        P(),
        P(),
        P(),
        P(),
        P(),
        P(),
        P(),
    )
    out_specs = (P("line", None, "gather", None), P(), P(), P(), P(), P(), P(), P(), P())
    return jax.shard_map(
        per_device, mesh=mesh, in_specs=in_specs, out_specs=out_specs, check_vma=False
    )
```

time: 376 us -> 137 us (0.36); the launches traced: 369 us -> 136 us
  waiting for transfers between devices: 127 us -> 0 us
  Pallas kernels: 0 us -> 85.3 us
  matrix products: 54.3 us -> 0.38 us
  blocking collectives: 46.9 us -> 0 us
  other arithmetic: 34.7 us -> 4.75 us
  local copies, waits for them, and re-layouts: 71.5 us -> 45.2 us
  starting transfers between devices: 19.3 us -> 0 us
  between operations: 15.1 us -> 0.85 us
    pallas_call x0 -> x3, Pallas kernels: none -> 85.3 us  [the longest x1 47.8 us: step(): pl.pallas_call(functools.partial(step_kernel, scale), out_shape=outs, in_...]
    psum x1 -> x0, waiting for transfers between devices: 81.4 us -> none  [per_device(): lax.psum((enc_grads[0], enc_grads[1], enc_grads[2], enc_grads[3], dec_cot...]
    dot_general x23 -> x1, matrix products: 54.3 us -> 0.38 us  [dot(): return jnp.dot(a, b, preferred_element_type=F32)]
    psum x1 -> x0, blocking collectives: 46.9 us -> none  [per_device(): lax.psum((enc_grads[0], enc_grads[1], enc_grads[2], enc_grads[3], dec_cot...]
    all_to_all x2 -> x0, waiting for transfers between devices: 46 us -> none  [the longest x1 40.1 us: per_device(): lax.all_to_all(latent, 'gather', split_axis=1, concat_axis=0, tiled=True)]
    another operation x1 -> x3, local copies, waits for them, and re-layouts: 19.9 us -> 0.31 us  [the longest x1 0.15 us: per_device(): gin_w.reshape(-1)]
    all_to_all x2 -> x0, starting transfers between devices: 19.2 us -> none  [the longest x1 11.3 us: per_device(): lax.all_to_all(dec_cots[0], 'gather', split_axis=0, concat_axis=1, tiled=...]
    reduce_sum x4 -> x7, other arithmetic: 15.7 us -> 2.83 us  [the longest x1 0.87 us: per_device(): gdb.sum(1)]
  transfers between devices with their start and end apart: 3 -> 0, of which waited for: 3 -> 0; matrix products, arithmetic and copies ran while one was open for 11% -> 0% of each run, Pallas kernels for 0% -> 0%
where the time goes in v1:
time: 137 us; the launch traced here: 136 us
  Pallas kernels  85.3 us (62%)
  local copies, waits for them, and re-layouts  45.2 us (33%)
  other arithmetic  4.75 us (3%)
    pallas_call x1, Pallas kernels, step(): pl.pallas_call(functools.partial(step_kernel, scale), out_shape=outs, in_...  47.8 us
    pallas_call x1, Pallas kernels, total(): pl.pallas_call(functools.partial(total_kernel, nd, n), out_shape=jax.Shap...  27.1 us
    slice x6, local copies, waits for them, and re-layouts, take(): return flat[at[0] - count:at[0]]  17 us
    pallas_call x1, Pallas kernels, exchange(): pl.pallas_call(functools.partial(exchange_kernel, n), out_shape=jax.Shape...  10.4 us
    unnamed x9, local copies, waits for them, and re-layouts  3.52 us

profile of v1, /device:TPU:0, one launch (start us, length us, event | category | flops | bytes accessed | tf_op | source)
XLA Modules:
  0.0 136.5 jit_solution(4991701365817932742)
XLA Ops:
  2.0 0.8 pad_maximum_fusion.x_ref
  2.9 10.4 %shard_map.169.a_ref = bf16[16,48,128]{2,1,0:T(8,128)(2,1)S(1)} custom-call(bf16[16,48,128]{2,1,0:T(8,128)(2,1)S(1)} %pad_maximum_fusion.x_ref), custom_call_target="tpu_custom_call" | custom-call | tf_op jit(solution)/shard_map/pallas_call | solution.py:60
  15.8 1.0 copy.47
  16.8 0.8 copy.52.w2_ref
  17.6 1.0 copy.48
  18.6 0.8 copy.53.w3_ref
  19.4 0.9 rev.6
  20.3 0.8 copy.54.v2_ref
  21.1 0.9 rev.7
  24.4 1.3 broadcast_in_dim.24.ib_ref
  25.7 1.3 broadcast_in_dim.25.mb_ref
  27.1 1.3 broadcast_in_dim.26.db_ref
  31.5 47.8 %shard_map.170 = (f32[16,16,256]{2,1,0:T(8,128)}, f32[192,192]{1,0:T(8,128)}, f32[192,192]{1,0:T(8,128)}, f32[640,48]{1,0:T(8,128)}, f32[32,512]{1,0:T(8,128)}, ...) custom-call(bf16[16,48,128]{2,1,0:T(8,128)(2,1)} %copy-done.1, f32[16,16,256]{2,1,0:T(8,128)} %bitcast.59, ...), custom_call_target="tpu_custom_call" | custom-call | flops 7247757312 | bytes 8388608 | tf_op jit(solution)/shard_map/pallas_call | solution.py:364
  79.3 1.0 reshape.193
  80.3 1.0 reshape.194
  81.4 1.1 copy.56
  83.0 1.2 slice_reduce_fusion
  84.3 0.9 reduce_sum.65
  85.2 0.9 reduce_sum.66
  86.1 0.9 reshape.196
  87.2 0.8 reduce_sum.68
  88.3 1.5 %concatenate.13 = f32[74436]{0:T(1024)S(1)} concatenate(f32[36864]{0:T(1024)S(1)} %reshape.193, f32[36864]{0:T(1024)S(1)} %reshape.194, f32[256]{0:T(256)S(1)} %reshape_reshape.6, f32[64]{0:T(128)S(1)} %reduce_sum.64, f32[64]{0:T(128)S(1)} %reduce_sum.65, f32[64]{0:T(128)S(1)} %reduce_sum.66, f32[256]{0:T(256)S(1)} %reshape_reshape.7, f32[4]{0:T(128)S(1)} %reshape.198), dimensions={0} | concatenate | bytes 595488 | tf_op jit(solution)/shard_map/concatenate | solution.py:447
  89.8 27.1 %shard_map.171 = f32[32,24,128]{2,1,0:T(8,128)S(1)} custom-call(f32[32,24,128]{2,1,0:T(8,128)S(1)} %bitcast.42), custom_call_target="tpu_custom_call" | custom-call | tf_op jit(solution)/shard_map/pallas_call | solution.py:148
  117.0 14.3 %slice.67 = f32[24576,4]{1,0:T(8,128)} reshape(f32[32,24,128]{2,1,0:T(8,128)S(1)} %shard_map.171) | data formatting | bytes 786432 | tf_op jit(solution)/shard_map/slice | solution.py:460
  (60 shorter events, 15.6 us)
Async XLA Ops:
  0.6 0.9 copy-start
  13.3 0.7 copy-start.1
  23.7 7.8 %copy-start.2 = (bf16[32,512]{1,0:T(8,128)(2,1)}, bf16[32,512]{1,0:T(8,128)(2,1)S(1)}, u32[]{:S(2)}) copy-start(bf16[32,512]{1,0:T(8,128)(2,1)S(1)} %reshape.191.wout_ref) | copy-start | bytes 98308

commit v2 on v1

--- a/solution.py
+++ b/solution.py
@@ -73,94 +73,141 @@
     )(x)
 
 
-def total_kernel(nd, n, x_ref, out_ref, held, result, send_sem, recv_sem, back_sem, done_sem):
-    me = lax.axis_index("line") * n + lax.axis_index("gather")
-
-    def at(peer):
-        return (peer // n, lax.rem(peer, n))
+def total_kernel(
+    chips, n, x_ref, out_ref, half, mine, held, result, pair_sem, send_sem, recv_sem, back_sem, done_sem, on_sem, end_sem
+):
+    flat = lax.axis_index("line") * n + lax.axis_index("gather")
+    chip = flat // 2
+    core = lax.rem(flat, 2)
+
+    def at(peer, which):
+        there = 2 * peer + which
+        return (there // n, lax.rem(there, n))
 
     barrier = pltpu.get_barrier_semaphore()
+    partner = at(chip, 1 - core)
+    pl.semaphore_signal(barrier, inc=1, device_id=partner, device_id_type=MESH)
 
     def greet(k, carry):
-        peer = lax.rem(me + k, nd)
-        pl.semaphore_signal(barrier, inc=1, device_id=at(peer), device_id_type=MESH)
-        return carry
-
-    lax.fori_loop(1, nd, greet, 0)
-    pl.semaphore_wait(barrier, nd - 1)
+        peer = lax.rem(chip + k, chips)
+        pl.semaphore_signal(barrier, inc=1, device_id=at(peer, core), device_id_type=MESH)
+        return carry
+
+    lax.fori_loop(1, chips, greet, 0)
+    pl.semaphore_wait(barrier, chips)
+
+    def remote(src, dst, send, recv, device):
+        return pltpu.make_async_remote_copy(
+            src_ref=src, dst_ref=dst, send_sem=send, recv_sem=recv, device_id=device, device_id_type=MESH
+        )
+
+    swap = remote(x_ref.at[1 - core], half, pair_sem.at[0], pair_sem.at[1], partner)
+    swap.start()
+    swap.wait()
+    mine[...] = x_ref[core] + half[...]
 
     def part(src, slot, peer, sem):
-        return pltpu.make_async_remote_copy(
-            src_ref=x_ref.at[src],
-            dst_ref=held.at[slot],
-            send_sem=send_sem.at[sem],
-            recv_sem=recv_sem.at[slot],
-            device_id=at(peer),
-            device_id_type=MESH,
-        )
+        return remote(mine.at[src], held.at[slot], send_sem.at[sem], recv_sem.at[slot], at(peer, core))
 
     def whole(slot, peer, sem):
-        return pltpu.make_async_remote_copy(
-            src_ref=result.at[slot],
-            dst_ref=result.at[slot],
-            send_sem=back_sem.at[sem],
-            recv_sem=done_sem.at[slot],
-            device_id=at(peer),
-            device_id_type=MESH,
-        )
+        where = result.at[core, slot]
+        return remote(where, where, back_sem.at[sem], done_sem.at[slot], at(peer, core))
+
+    def over(which, slot):
+        where = result.at[which, slot]
+        return remote(where, where, on_sem.at[slot], end_sem.at[slot], partner)
 
     def send(k, carry):
-        peer = lax.rem(me + k, nd)
-        part(peer, me, peer, k).start()
-        return carry
-
-    lax.fori_loop(1, nd, send, 0)
+        peer = lax.rem(chip + k, chips)
+        part(peer, chip, peer, k).start()
+        return carry
+
+    lax.fori_loop(1, chips, send, 0)
 
     def add(k, acc):
-        source = lax.rem(me + nd - k, nd)
+        source = lax.rem(chip + chips - k, chips)
         part(source, source, source, k).wait_recv()
-        return acc + held[pl.ds(source, 1)]
-
-    result[pl.ds(me, 1)] = lax.fori_loop(1, nd, add, x_ref[pl.ds(me, 1)])
+        return acc + held[source]
+
+    result[core, chip] = lax.fori_loop(1, chips, add, mine[chip])
 
     def spread(k, carry):
-        peer = lax.rem(me + k, nd)
-        whole(me, peer, k).start()
-        return carry
-
-    lax.fori_loop(1, nd, spread, 0)
+        peer = lax.rem(chip + k, chips)
+        whole(chip, peer, k).start()
+        return carry
+
+    lax.fori_loop(1, chips, spread, 0)
+    over(core, chip).start()
+
+    def forward(k, carry):
+        source = lax.rem(chip + chips - k, chips)
+        whole(source, source, k).wait_recv()
+        over(core, source).start()
+        return carry
+
+    lax.fori_loop(1, chips, forward, 0)
 
     def finish(k, carry):
-        peer = lax.rem(me + k, nd)
-        source = lax.rem(me + nd - k, nd)
-        part(peer, me, peer, k).wait_send()
-        whole(me, peer, k).wait_send()
-        whole(source, peer, k).wait_recv()
-        return carry
-
-    lax.fori_loop(1, nd, finish, 0)
+        peer = lax.rem(chip + k, chips)
+        part(peer, chip, peer, k).wait_send()
+        whole(chip, peer, k).wait_send()
+        return carry
+
+    lax.fori_loop(1, chips, finish, 0)
+
+    def close(k, carry):
+        over(core, k).wait_send()
+        over(1 - core, k).wait_recv()
+        return carry
+
+    lax.fori_loop(0, chips, close, 0)
     out_ref[...] = result[...]
 
 
 def total(x, n):
-    nd = x.shape[0]
-    sems = pltpu.SemaphoreType.DMA((nd,))
+    chips, per, wide = x.shape[1:]
+    sems = pltpu.SemaphoreType.DMA((chips,))
+    part = pltpu.VMEM((chips, per, wide), F32)
     return pl.pallas_call(
-        functools.partial(total_kernel, nd, n),
+        functools.partial(total_kernel, chips, n),
         out_shape=jax.ShapeDtypeStruct(x.shape, x.dtype),
         in_specs=[pl.BlockSpec(memory_space=pltpu.VMEM)],
         out_specs=pl.BlockSpec(memory_space=pltpu.VMEM),
-        scratch_shapes=[
-            pltpu.VMEM(x.shape, x.dtype),
-            pltpu.VMEM(x.shape, x.dtype),
-            sems,
-            sems,
-            sems,
-            sems,
-        ],
+        scratch_shapes=[part, part, part, pltpu.VMEM(x.shape, F32), pltpu.SemaphoreType.DMA((2,))]
+        + [sems] * 6,
         compiler_params=pltpu.CompilerParams(
             collective_id=1, has_side_effects=True, vmem_limit_bytes=16 << 20
         ),
+    )(x)
+
+
+def unpack_kernel(x_ref, in_w_ref, in_b_ref, mid_w_ref, mid_b_ref, dec_w_ref, dec_b_ref, out_w_ref, out_b_ref):
+    c = in_w_ref.shape[0]
+    for a in range(3):
+        for b in range(3):
+            for first, ref in ((0, mid_w_ref), (3, dec_w_ref)):
+                tile, side = (first + a) // 2, (first + a) % 2
+                row = tile * 3 * c + b * c
+                ref[a, b] = x_ref[row : row + c, side * c : (side + 1) * c]
+    small = x_ref[9 * c : 10 * c]
+    in_w_ref[...] = small[:, 0:4]
+    flipped = small.T
+    in_b_ref[...] = flipped[4:5]
+    mid_b_ref[...] = flipped[5:6]
+    dec_b_ref[...] = flipped[6:7]
+    out_w_ref[...] = flipped[8:12]
+    out_b_ref[...] = flipped[12:13, 0:4]
+
+
+def unpack(x, c):
+    vmem = pl.BlockSpec(memory_space=pltpu.VMEM)
+    sizes = ((c, 4), (1, c), (3, 3, c, c), (1, c), (3, 3, c, c), (1, c), (4, c), (1, 4))
+    return pl.pallas_call(
+        unpack_kernel,
+        out_shape=tuple(jax.ShapeDtypeStruct(size, F32) for size in sizes),
+        in_specs=[vmem],
+        out_specs=(vmem,) * len(sizes),
+        compiler_params=pltpu.CompilerParams(vmem_limit_bytes=16 << 20),
     )(x)
 
 
@@ -190,7 +237,27 @@
     scale,
     a_ref,
     target_ref,
+    in_w_ref,
+    in_b_ref,
+    mid_w_ref,
+    mid_b_ref,
+    dec_w_ref,
+    dec_b_ref,
+    out_w_ref,
+    out_b_ref,
+    res_ref,
+    pack_ref,
+    h_ref,
+    z_ref,
+    e3_ref,
+    e2_ref,
+    e1_ref,
+    h3_ref,
+    s1_ref,
+    s2_ref,
+    s3_ref,
     win_ref,
+    wide_ref,
     w2_ref,
     w3_ref,
     v2_ref,
@@ -201,10 +268,8 @@
     mb_ref,
     db_ref,
     ob_ref,
-    edge_ref,
     deint_ref,
     inter_ref,
-    res_ref,
     g2_ref,
     g3_ref,
     gin_ref,
@@ -212,21 +277,57 @@
     gob_ref,
     gmb_ref,
     gdb_ref,
-    h_ref,
-    z_ref,
-    e3_ref,
-    e2_ref,
-    e1_ref,
-    h3_ref,
-    s1_ref,
-    s2_ref,
-    s3_ref,
 ):
     shots, rows = target_ref.shape[0], target_ref.shape[1]
     rl = rows // 2
     hr = rl + 2
     c = ib_ref.shape[0]
     t = ib_ref.shape[1]
+    ka = a_ref.shape[1]
+
+    def grid(height, width):
+        return (
+            lax.broadcasted_iota(jnp.int32, (height, width), 0),
+            lax.broadcasted_iota(jnp.int32, (height, width), 1),
+        )
+
+    def onehot(mask):
+        return jnp.where(mask, 1.0, 0.0).astype(BF)
+
+    for src, fwd, back in ((mid_w_ref, w2_ref, v2_ref), (dec_w_ref, w3_ref, v3_ref)):
+        for q in range(9):
+            wide_ref[:, q * c : (q + 1) * c] = src[q // 3, q % 3].astype(F32)
+        fwd[...] = wide_ref[...].astype(BF)
+        for q in range(9):
+            wide_ref[:, q * c : (q + 1) * c] = src[2 - q // 3, q % 3].astype(F32).T
+        back[...] = wide_ref[...].astype(BF)
+    for src, dst in ((in_b_ref, ib_ref), (mid_b_ref, mb_ref), (dec_b_ref, db_ref)):
+        dst[...] = jnp.broadcast_to(src[...], (t, c)).T
+    row, col = grid(4, ka)
+    for r in range(hr):
+        spot = onehot(col == lax.rem(row, 2) * 2 * hr + 2 * r + row // 2)
+        win_ref[r * c : (r + 1) * c] = dot(in_w_ref[...], spot).astype(BF)
+    row, col = grid(4, 2 * rows)
+    for r in range(rl):
+        spot = onehot(col == lax.rem(row, 2) * rows + 2 * r + row // 2).astype(F32)
+        block = lax.dot_general(
+            out_w_ref[...].astype(F32), spot, (((0,), (0,)), ((), ())), preferred_element_type=F32
+        )
+        woutt_ref[r * c : (r + 1) * c] = block.astype(BF)
+    wout_ref[...] = woutt_ref[...].astype(F32).T.astype(BF)
+    row, col = grid(2 * rows, t)
+    sample = lax.rem(row, 2) * 2 + row // rows
+    spread = jnp.zeros((2 * rows, t), F32)
+    for k in range(4):
+        spread = jnp.where(sample == k, out_b_ref[0:1, k : k + 1], spread)
+    ob_ref[...] = spread
+    row, col = grid(2 * t, 2 * t)
+    deint_ref[...] = onehot(row == 2 * lax.rem(col, t) + col // t)
+    inter_ref[...] = onehot(col == 2 * lax.rem(row, t) + row // t)
+    me = lax.axis_index("gather")
+    low = jnp.where(me > 0, 1.0, 0.0)
+    high = jnp.where(me < shots - 1, 1.0, 0.0)
+
     lane = lax.broadcasted_iota(jnp.int32, (c, t), 1)
     first, last = lane == 0, lane == t - 1
 
@@ -253,9 +354,9 @@
         for r in range(hr):
             act, slope = gate(pre1[r * c : (r + 1) * c] + ib_ref[...])
             if r == 0:
-                act, slope = act * edge_ref[0:1], slope * edge_ref[0:1]
+                act, slope = act * low, slope * low
             if r == hr - 1:
-                act, slope = act * edge_ref[1:2], slope * edge_ref[1:2]
+                act, slope = act * high, slope * high
             s1_ref[s, r] = slope
             h_ref[s, r, 0:c] = later(act)
             h_ref[s, r, c : 2 * c] = act.astype(BF)
@@ -293,7 +394,7 @@
         g = resid * scale
         gob_ref[...] += g
         g = g.astype(BF)
-        gout_ref[...] += dot_t(g, h3_ref[...])
+        gout_ref[...] += dot_t(h3_ref[...], g)
         back3 = dot(woutt_ref[...], g)
         bias = gdb_ref[...]
         for r in range(rl):
@@ -344,42 +445,88 @@
 
     lax.fori_loop(0, shots, pull, 0)
 
-
-def step(scale, operands, shots, rows, c, t, ka):
+    both = jnp.concatenate([g2_ref[...], g3_ref[...]], axis=1)
+    for tile in range(3):
+        pack_ref[tile * 3 * c : (tile + 1) * 3 * c] = both[:, tile * t : (tile + 1) * t]
+    small = jnp.zeros((c, t), F32)
+    row, col = grid(ka, t)
+    for r in range(hr):
+        spot = onehot(
+            ((row == lax.rem(col, 2) * 2 * hr + 2 * r + col // 2) & (col < 4))
+            | ((row == 4 * hr) & (col == 4))
+        )
+        small = small + exact_dot(gin_ref[r * c : (r + 1) * c], spot)
+    row, col = grid(2 * rows, t)
+    k = col - 8
+    for r in range(rl):
+        spot = onehot(
+            (k >= 0) & (k < 4) & (row == lax.rem(col, 2) * rows + 2 * r + k // 2)
+        )
+        small = small + exact_dot(gout_ref[r * c : (r + 1) * c], spot)
+    row, col = grid(c, t)
+    small = jnp.where(col == 5, jnp.sum(gmb_ref[...], axis=1, keepdims=True), small)
+    small = jnp.where(col == 6, jnp.sum(gdb_ref[...], axis=1, keepdims=True), small)
+    gob = jnp.sum(gob_ref[...], axis=1, keepdims=True)
+    for k in range(4):
+        one = jnp.sum(jnp.where(sample[:, 0:1] == k, gob, 0.0), axis=0, keepdims=True)
+        small = jnp.where((col == 12) & (row == k), one, small)
+    pack_ref[9 * c : 10 * c] = small
+    spare = pack_ref.shape[0] - 10 * c
+    if spare:
+        pack_ref[10 * c :] = jnp.zeros((spare, t), F32)
+
+
+def step(scale, operands, shots, rows, c, t, ka, packed):
     rl = rows // 2
     hr = rl + 2
     vmem = pl.BlockSpec(memory_space=pltpu.VMEM)
-    shape = jax.ShapeDtypeStruct
     outs = (
-        shape((shots, rows, 2 * t), F32),
-        shape((3 * c, 3 * c), F32),
-        shape((3 * c, 3 * c), F32),
-        shape((hr * c, ka), F32),
-        shape((2 * rows, rl * c), F32),
-        shape((2 * rows, t), F32),
-        shape((c, t), F32),
-        shape((c, t), F32),
+        jax.ShapeDtypeStruct((shots, rows, 2 * t), F32),
+        jax.ShapeDtypeStruct((packed, t), F32),
     )
-    flops = 2 * 6 * 9 * c * c * shots * rl * t
+    scratch = [
+        ((shots, hr, 3 * c, t), BF),
+        ((rl, shots + 2, 3 * c, t), BF),
+        ((rl, shots + 2, 3 * c, t), BF),
+        ((rl + 4, 3 * c, t), BF),
+        ((hr * c, t), BF),
+        ((rl * c, t), BF),
+        ((shots, hr, c, t), F32),
+        ((shots, rl, c, t), F32),
+        ((rl, c, t), F32),
+        ((hr * c, ka), BF),
+        ((c, 9 * c), F32),
+        ((c, 9 * c), BF),
+        ((c, 9 * c), BF),
+        ((c, 9 * c), BF),
+        ((c, 9 * c), BF),
+        ((2 * rows, rl * c), BF),
+        ((rl * c, 2 * rows), BF),
+        ((c, t), F32),
+        ((c, t), F32),
+        ((c, t), F32),
+        ((2 * rows, t), F32),
+        ((2 * t, 2 * t), BF),
+        ((2 * t, 2 * t), BF),
+        ((3 * c, 3 * c), F32),
+        ((3 * c, 3 * c), F32),
+        ((hr * c, ka), F32),
+        ((rl * c, 2 * rows), F32),
+        ((2 * rows, t), F32),
+        ((c, t), F32),
+        ((c, t), F32),
+    ]
     return pl.pallas_call(
         functools.partial(step_kernel, scale),
         out_shape=outs,
         in_specs=[vmem] * len(operands),
         out_specs=(vmem,) * len(outs),
-        scratch_shapes=[
-            pltpu.VMEM((shots, hr, 3 * c, t), BF),
-            pltpu.VMEM((rl, shots + 2, 3 * c, t), BF),
-            pltpu.VMEM((rl, shots + 2, 3 * c, t), BF),
-            pltpu.VMEM((rl + 4, 3 * c, t), BF),
-            pltpu.VMEM((hr * c, t), BF),
-            pltpu.VMEM((rl * c, t), BF),
-            pltpu.VMEM((shots, hr, c, t), F32),
-            pltpu.VMEM((shots, rl, c, t), F32),
-            pltpu.VMEM((rl, c, t), F32),
-        ],
+        scratch_shapes=[pltpu.VMEM(size, kind) for size, kind in scratch],
         compiler_params=pltpu.CompilerParams(vmem_limit_bytes=56 << 20),
         cost_estimate=pl.CostEstimate(
-            flops=flops, bytes_accessed=8 << 20, transcendentals=3 * c * shots * rl * t
+            flops=2 * 6 * 9 * c * c * shots * rl * t,
+            bytes_accessed=2 << 20,
+            transcendentals=3 * c * shots * rl * t,
         ),
     )(*operands)
 
@@ -392,12 +539,10 @@
     c, t, rl = in_w.shape[0], nt // 2, rows // 2
     hr = rl + 2
     scale = 1.0 / math.sqrt(lines * n * recv * nt)
-    me = lax.axis_index("gather")
     ka = -(-(4 * hr + 1) // 16) * 16
 
     when = jnp.arange(nt)
     deint = (when[:, None] == (2 * (when % t) + when // t)[None, :]).astype(BF)
-    inter = deint.T
     wanted = (jnp.arange(n)[:, None] * rows + jnp.arange(2 * hr)[None, :] - 2).reshape(-1)
     select = (wanted[:, None] == jnp.arange(recv)[None, :]).astype(BF)
     picked = dot(select, noisy[0, 0]).astype(BF)
@@ -406,73 +551,32 @@
     blocks = jnp.concatenate([picked[..., :t], picked[..., t:], tail], axis=1)
     cells = exchange(blocks)
 
-    iw = in_w.reshape(c, 2, 2)
-    win = jnp.einsum("rq,dij->rdjqi", jnp.eye(hr, dtype=BF), iw).reshape(hr * c, 4 * hr)
-    win = jnp.pad(win, ((0, 0), (0, ka - 4 * hr)))
-    ow = out_w.reshape(2, 2, c)
-    wout = jnp.einsum("rq,ijd->jqird", jnp.eye(rl, dtype=BF), ow).reshape(2 * rows, rl * c)
-    ob = jnp.broadcast_to(out_b.reshape(2, 2).T[:, None, :], (2, rl, 2)).reshape(2 * rows, 1)
-    w2 = mid_w.transpose(2, 0, 1, 3).reshape(c, 9 * c)
-    w3 = dec_w.transpose(2, 0, 1, 3).reshape(c, 9 * c)
-    v2 = mid_w[::-1].transpose(3, 0, 1, 2).reshape(c, 9 * c)
-    v3 = dec_w[::-1].transpose(3, 0, 1, 2).reshape(c, 9 * c)
-    edge = jnp.stack([me > 0, me < n - 1]).astype(F32)
+    per = -(-10 * c // (8 * nd)) * 8
     operands = (
         cells,
         target[0],
-        win,
-        w2,
-        w3,
-        v2,
-        v3,
-        wout,
-        wout.T,
-        jnp.broadcast_to(in_b[:, None], (c, t)),
-        jnp.broadcast_to(mid_b[:, None], (c, t)),
-        jnp.broadcast_to(dec_b[:, None], (c, t)),
-        jnp.broadcast_to(ob, (2 * rows, t)),
-        jnp.broadcast_to(edge[:, None], (2, t)),
-        deint,
-        inter,
+        in_w,
+        in_b[None],
+        mid_w,
+        mid_b[None],
+        dec_w,
+        dec_b[None],
+        out_w,
+        out_b[None],
     )
-    res, g2, g3, gin, gout, gob, gmb, gdb = step(scale, operands, shots, rows, c, t, ka)
-
-    gin_w = jnp.einsum("rdjri->dij", gin[:, : 4 * hr].reshape(hr, c, 2, hr, 2)).reshape(c, 4)
-    gin_b = gin[:, 4 * hr].reshape(hr, c).sum(0)
-    gout_w = jnp.einsum("jrird->ijd", gout.reshape(2, rl, 2, rl, c)).reshape(4, c)
-    gout_b = gob.sum(1).reshape(2, rl, 2).sum(1).T.reshape(4)
-    small = jnp.concatenate(
-        [gin_w.reshape(-1), gin_b, gmb.sum(1), gdb.sum(1), gout_w.reshape(-1), gout_b]
-    )
-    flat = jnp.concatenate([g2.reshape(-1), g3.reshape(-1), small])
-    per = -(-flat.shape[0] // (nd * 8 * 128)) * 8
-    flat = jnp.pad(flat, (0, nd * per * 128 - flat.shape[0])).reshape(nd, per, 128)
-    flat = total(flat, n).reshape(-1)
-
-    def taps(part):
-        return part.reshape(3, c, 3, c).transpose(2, 0, 1, 3)
-
-    big = 9 * c * c
-    at = [2 * big]
-
-    def take(count):
-        at[0] += count
-        return flat[at[0] - count : at[0]]
-
-    din_w = take(4 * c).reshape(c, 4)
-    din_b, dmid_b, ddec_b = take(c), take(c), take(c)
-    dout_w = take(4 * c).reshape(4, c)
-    dout_b = take(4)
+    res, pack = step(scale, operands, shots, rows, c, t, ka, nd * per)
+    pack = total(pack.reshape(2, nd // 2, per, t), n).reshape(nd * per, t)
+    din_w, din_b, dmid_w, dmid_b, ddec_w, ddec_b, dout_w, dout_b = unpack(pack, c)
     return (
         res[None],
         din_w,
-        din_b,
-        taps(flat[:big]),
-        dmid_b,
-        taps(flat[big : 2 * big]),
-        ddec_b,
+        din_b[0],
+        dmid_w,
+        dmid_b[0],
+        ddec_w,
+        ddec_b[0],
         dout_w,
-        dout_b,
+        dout_b[0],
     )
 
 

time: 137 us -> 87.3 us (0.64)
  local copies, waits for them, and re-layouts: 45.2 us -> 4.5 us
  other arithmetic: 4.75 us -> 0.13 us
  Pallas kernels: 85.3 us -> 81.3 us
    slice x9 -> x0, local copies, waits for them, and re-layouts: 19.4 us -> none  [the longest x6 17 us: take(): return flat[at[0] - count:at[0]]]
    reshape x19 -> x0, local copies, waits for them, and re-layouts: 9.98 us -> none  [the longest x2 2.09 us: per_device(): flat = jnp.concatenate([g2.reshape(-1), g3.reshape(-1), small])]
    broadcast_in_dim x7 -> x0, local copies, waits for them, and re-layouts: 5.39 us -> none  [the longest x1 1.33 us: per_device(): jnp.broadcast_to(mid_b[:, None], (c, t))]
    pallas_call x1 -> x2, Pallas kernels: 27.1 us -> 22 us  [the longest x1 21 us: total(): pl.pallas_call(functools.partial(total_kernel, chips, n), out_shape=jax.S...]
    reduce_sum x7 -> x0, other arithmetic: 2.83 us -> none  [the longest x1 0.87 us: per_device(): gdb.sum(1)]
    transpose x6 -> x0, local copies, waits for them, and re-layouts: 2.4 us -> none  [the longest x1 1.05 us: per_device(): w2 = mid_w.transpose(2, 0, 1, 3).reshape(c, 9 * c)]
    rev x2 -> x0, local copies, waits for them, and re-layouts: 1.84 us -> none  [the longest x1 0.92 us: per_device(): v2 = mid_w[::-1].transpose(3, 0, 1, 2).reshape(c, 9 * c)]
    concatenate x1 -> x0, local copies, waits for them, and re-layouts: 1.47 us -> none  [per_device(): flat = jnp.concatenate([g2.reshape(-1), g3.reshape(-1), small])]
where the time goes in v2:
time: 87.3 us; the launch traced here: 87.1 us
  Pallas kernels  81.3 us (93%)
  local copies, waits for them, and re-layouts  4.5 us (5%)
    pallas_call x1, Pallas kernels, step(): pl.pallas_call(functools.partial(step_kernel, scale), out_shape=outs, in_...  48.9 us
    pallas_call x1, Pallas kernels, total(): pl.pallas_call(functools.partial(total_kernel, chips, n), out_shape=jax.S...  21 us
    pallas_call x1, Pallas kernels, exchange(): pl.pallas_call(functools.partial(exchange_kernel, n), out_shape=jax.Shape...  10.4 us
    unnamed x12, local copies, waits for them, and re-layouts  4.34 us

profile of v2, /device:TPU:0, one launch (start us, length us, event | category | flops | bytes accessed | tf_op | source)
XLA Modules:
  0.0 87.1 jit_solution(9939404672945183155)
XLA Ops:
  0.6 0.0 copy-start
  0.7 0.1 add_add_fusion
  0.8 0.0 copy-start.4
  0.8 0.1 sub.13
  0.8 0.6 copy-done.4
  1.4 0.7 copy.21.in_w_ref
  2.1 0.0 copy-done
  2.1 0.4 convolution_convert_fusion
  2.6 0.0 copy-start.3
  2.6 0.7 copy-done.3
  3.3 0.1 pad_maximum_fusion.x_ref
  3.4 10.4 %shard_map.169.a_ref = bf16[16,48,128]{2,1,0:T(8,128)(2,1)S(1)} custom-call(bf16[16,48,128]{2,1,0:T(8,128)(2,1)S(1)} %pad_maximum_fusion.x_ref), custom_call_target="tpu_custom_call" | custom-call | tf_op jit(solution)/shard_map/pallas_call | solution.py:60
  13.8 0.0 copy-start.2
  13.8 0.7 copy-done.2
  14.5 48.9 %shard_map.170 = (f32[16,16,256]{2,1,0:T(8,128)}, f32[768,128]{1,0:T(8,128)}) custom-call(bf16[16,48,128]{2,1,0:T(8,128)(2,1)} %copy-done.2, f32[16,16,256]{2,1,0:T(8,128)} %bitcast.18, bf16[64,4]{1,0:T(8,128)(2,1)} %copy.21.in_w_ref, f32[1,64]{1,0:T(1,128)} %bitcast.19, bf16[3,3,64,64]{3,2,1,0:T(8,128)(2,1)} %mid_w_ref.1, f32[1,64]{1,0:T(1,128)} %bitcast.20, ...), custom_call_target="tpu_custom_call" | custom-call | flops 7247757312 | bytes 2097152 | tf_op jit(solution)/shard_map/pallas_call | solution.py:519
  63.4 0.0 copy-start.1
  63.4 1.0 %copy-done.1 = f32[768,128]{1,0:T(8,128)S(1)} copy-done((f32[768,128]{1,0:T(8,128)S(1)}, f32[768,128]{1,0:T(8,128)}, u32[]{:S(2)}) %copy-start.1) | copy-done | bytes 393240
  64.4 21.0 %shard_map.171 = f32[2,16,24,128]{3,2,1,0:T(8,128)S(1)} custom-call(f32[2,16,24,128]{3,2,1,0:T(8,128)S(1)} %bitcast.17), custom_call_target="tpu_custom_call" | custom-call | tf_op jit(solution)/shard_map/pallas_call | solution.py:171
  85.5 0.9 %shard_map.172 = (f32[64,4]{1,0:T(8,128)S(1)}, f32[1,64]{1,0:T(1,128)}, f32[3,3,64,64]{3,2,1,0:T(8,128)}, f32[1,64]{1,0:T(1,128)}, f32[3,3,64,64]{3,2,1,0:T(8,12...) custom-call(f32[768,128]{1,0:T(8,128)S(1)} %bitcast.16), custom_call_target="tpu_custom_call" | custom-call | tf_op jit(solution)/shard_map/pallas_call | solution.py:205
  86.4 0.7 copy.22
  (4 shorter events, 0.1 us)
Async XLA Ops:
  0.6 1.5 %copy-start = (bf16[1,1,256,256]{3,2,1,0:T(8,128)(2,1)S(1)}, bf16[1,1,256,256]{3,2,1,0:T(8,128)(2,1)}, u32[]{:S(2)}) copy-start(bf16[1,1,256,256]{3,2,1,0:T(8,128)(2,1)} %param.12) | copy-start | bytes 393220
  0.8 0.7 copy-start.4
  2.6 0.8 copy-start.3
  13.8 0.7 copy-start.2
  63.4 1.0 %copy-start.1 = (f32[768,128]{1,0:T(8,128)S(1)}, f32[768,128]{1,0:T(8,128)}, u32[]{:S(2)}) copy-start(f32[768,128]{1,0:T(8,128)} %get-tuple-element.32) | copy-start | bytes 1179652

commit v3 on v2

--- a/solution.py
+++ b/solution.py
@@ -212,7 +212,7 @@
 
 
 def gate(pre):
-    sig = 1.0 / (1.0 + jnp.exp(-pre))
+    sig = 0.5 * jnp.tanh(0.5 * pre) + 0.5
     act = pre * sig
     return act, sig + act * (1.0 - sig)
 
@@ -230,7 +230,10 @@
     rest = x - hi.astype(F32)
     mid = rest.astype(BF)
     low = (rest - mid.astype(F32)).astype(BF)
-    return dot(hi, onehot) + dot(mid, onehot) + dot(low, onehot)
+    size = x.shape[0]
+    pieces = jnp.concatenate([hi.astype(F32), mid.astype(F32), low.astype(F32)], axis=0).astype(BF)
+    out = dot(pieces, onehot)
+    return out[:size] + out[size : 2 * size] + out[2 * size :]
 
 
 def step_kernel(
@@ -332,10 +335,10 @@
     first, last = lane == 0, lane == t - 1
 
     def later(x):
-        return jnp.where(first, 0.0, pltpu.roll(x, 1, 1)).astype(BF)
+        return jnp.where(first, jnp.zeros((), BF), pltpu.roll(x.astype(BF), 1, 1))
 
     def sooner(x):
-        return jnp.where(last, 0.0, pltpu.roll(x, t - 1, 1)).astype(BF)
+        return jnp.where(last, jnp.zeros((), BF), pltpu.roll(x.astype(BF), t - 1, 1))
 
     def band(ref, r):
         return ref[r : r + 3].reshape(3 * 3 * c, t)
@@ -374,7 +377,7 @@
                 z_ref[r + q, s + 1, 2 * c : 3 * c] = sooner(act)
         return carry
 
-    lax.fori_loop(0, shots, encode, 0)
+    lax.fori_loop(0, shots, encode, 0, unroll=8)
 
     def decode(s, carry):
         for r in range(0, rl, 2):
@@ -411,7 +414,7 @@
         g3_ref[...] += dot_t(left, right)
         return carry
 
-    lax.fori_loop(0, shots, decode, 0)
+    lax.fori_loop(0, shots, decode, 0, unroll=8)
 
     def pull(s, carry):
         bias = gmb_ref[...]
@@ -443,7 +446,7 @@
         gin_ref[...] += dot_t(e1_ref[...], a_ref[s])
         return carry
 
-    lax.fori_loop(0, shots, pull, 0)
+    lax.fori_loop(0, shots, pull, 0, unroll=8)
 
     both = jnp.concatenate([g2_ref[...], g3_ref[...]], axis=1)
     for tile in range(3):

time: 87.3 us -> 74.8 us (0.86)
  Pallas kernels: 81.3 us -> 68.8 us
    pallas_call x1, Pallas kernels: 48.9 us -> 36.4 us  [step(): pl.pallas_call(functools.partial(step_kernel, scale), out_shape=outs, in_...]
where the time goes in v3:
time: 74.8 us; the launch traced here: 74.5 us
  Pallas kernels  68.8 us (92%)
  local copies, waits for them, and re-layouts  4.5 us (6%)
    pallas_call x1, Pallas kernels, step(): pl.pallas_call(functools.partial(step_kernel, scale), out_shape=outs, in_...  36.4 us
    pallas_call x1, Pallas kernels, total(): pl.pallas_call(functools.partial(total_kernel, chips, n), out_shape=jax.S...  21 us
    pallas_call x1, Pallas kernels, exchange(): pl.pallas_call(functools.partial(exchange_kernel, n), out_shape=jax.Shape...  10.4 us
    unnamed x12, local copies, waits for them, and re-layouts  4.34 us

profile of v3, /device:TPU:0, one launch (start us, length us, event | category | flops | bytes accessed | tf_op | source)
XLA Modules:
  0.0 74.5 jit_solution(10605838798728932689)
XLA Ops:
  0.6 0.0 copy-start
  0.7 0.1 add_add_fusion
  0.8 0.0 copy-start.4
  0.8 0.1 sub.13
  0.8 0.6 copy-done.4
  1.4 0.7 copy.21.in_w_ref
  2.1 0.0 copy-done
  2.1 0.4 convolution_convert_fusion
  2.6 0.0 copy-start.3
  2.6 0.7 copy-done.3
  3.3 0.1 pad_maximum_fusion.x_ref
  3.4 10.4 %shard_map.169.a_ref = bf16[16,48,128]{2,1,0:T(8,128)(2,1)S(1)} custom-call(bf16[16,48,128]{2,1,0:T(8,128)(2,1)S(1)} %pad_maximum_fusion.x_ref), custom_call_target="tpu_custom_call" | custom-call | tf_op jit(solution)/shard_map/pallas_call | solution.py:60
  13.8 0.0 copy-start.2
  13.8 0.7 copy-done.2
  14.5 36.4 %shard_map.170 = (f32[16,16,256]{2,1,0:T(8,128)}, f32[768,128]{1,0:T(8,128)}) custom-call(bf16[16,48,128]{2,1,0:T(8,128)(2,1)} %copy-done.2, f32[16,16,256]{2,1,0:T(8,128)} %bitcast.18, bf16[64,4]{1,0:T(8,128)(2,1)} %copy.21.in_w_ref, f32[1,64]{1,0:T(1,128)} %bitcast.19, bf16[3,3,64,64]{3,2,1,0:T(8,128)(2,1)} %mid_w_ref.1, f32[1,64]{1,0:T(1,128)} %bitcast.20, ...), custom_call_target="tpu_custom_call" | custom-call | flops 7247757312 | bytes 2097152 | tf_op jit(solution)/shard_map/pallas_call | solution.py:522
  50.9 0.0 copy-start.1
  50.9 1.0 %copy-done.1 = f32[768,128]{1,0:T(8,128)S(1)} copy-done((f32[768,128]{1,0:T(8,128)S(1)}, f32[768,128]{1,0:T(8,128)}, u32[]{:S(2)}) %copy-start.1) | copy-done | bytes 393240
  51.9 21.0 %shard_map.171 = f32[2,16,24,128]{3,2,1,0:T(8,128)S(1)} custom-call(f32[2,16,24,128]{3,2,1,0:T(8,128)S(1)} %bitcast.17), custom_call_target="tpu_custom_call" | custom-call | tf_op jit(solution)/shard_map/pallas_call | solution.py:171
  72.9 0.9 %shard_map.172 = (f32[64,4]{1,0:T(8,128)S(1)}, f32[1,64]{1,0:T(1,128)}, f32[3,3,64,64]{3,2,1,0:T(8,128)}, f32[1,64]{1,0:T(1,128)}, f32[3,3,64,64]{3,2,1,0:T(8,12...) custom-call(f32[768,128]{1,0:T(8,128)S(1)} %bitcast.16), custom_call_target="tpu_custom_call" | custom-call | tf_op jit(solution)/shard_map/pallas_call | solution.py:205
  73.9 0.7 copy.22
  (4 shorter events, 0.1 us)
Async XLA Ops:
  0.6 1.5 %copy-start = (bf16[1,1,256,256]{3,2,1,0:T(8,128)(2,1)S(1)}, bf16[1,1,256,256]{3,2,1,0:T(8,128)(2,1)}, u32[]{:S(2)}) copy-start(bf16[1,1,256,256]{3,2,1,0:T(8,128)(2,1)} %param.12) | copy-start | bytes 393220
  0.8 0.7 copy-start.4
  2.6 0.8 %copy-start.3 = (bf16[16,8,128]{2,1,0:T(8,128)(2,1)S(1)}, bf16[16,8,128]{2,1,0:T(8,128)(2,1)}, u32[]{:S(2)}) copy-start(bf16[16,8,128]{2,1,0:T(8,128)(2,1)} %constant.67.clone.1) | copy-start | bytes 98308
  13.8 0.7 copy-start.2
  50.9 1.0 %copy-start.1 = (f32[768,128]{1,0:T(8,128)S(1)}, f32[768,128]{1,0:T(8,128)}, u32[]{:S(2)}) copy-start(f32[768,128]{1,0:T(8,128)} %get-tuple-element.32) | copy-start | bytes 1179652
